TPU v7x, 512 devices: a whole 4x4x16 slice. The times are simulated.
512 devices in a mesh: ctx: 16 (over z), exp: 32 (over y, x, core).
Axes of the slice: x: 4, y: 4, z: 16, core: 2. Of those that a mesh axis runs over, the one named last changes fastest.
Arguments:
- queries: bfloat16 [1024, 4096], P('ctx', 'exp'), may hold values from -36 to 36
- keys: bfloat16 [1024, 1024], P('ctx'), may hold values from -4 to 4
- values: bfloat16 [1024, 1024], P('ctx'), may hold values from -6 to 6
- out_proj: bfloat16 [4096, 4096], P('ctx', 'exp'), may hold values from -0.09375 to 0.09375
- residual_in: bfloat16 [1024, 4096], P('ctx', 'exp'), may hold values from -48 to 48
- norm_gain: float32 [4096], P('exp'), may hold values from 0.1 to 1.9
- routes: int32 [1024, 2], replicated, may hold values from 0 to 7, all different within a row; in each aligned block of 64 rows (0 to 63, 64 to 127, ...) at most 16 rows name the same one
- gate_wts: float32 [1024, 2], P('ctx'), may hold values from 0.2 to 1
- w_gate: bfloat16 [4096, 65536], P(None, ('exp', 'ctx')), may hold values from -0.09375 to 0.09375
- w_up: bfloat16 [4096, 65536], P(None, ('exp', 'ctx')), may hold values from -0.09375 to 0.09375
- w_down: bfloat16 [65536, 4096], P(('exp', 'ctx')), may hold values from -0.25 to 0.25
Outputs:
- residual_out: bfloat16 [1024, 4096], P('ctx', 'exp')
- expert_out: bfloat16 [1024, 4096], P('ctx', 'exp')
Inputs may be any that keep to these rules, and one draw needn't show every extreme that they name: `routes`: within the 64 tokens of one ctx shard no expert is named more than 16 times, and in every draw some expert is named exactly 16 times within some shard; the two experts of a token differ.
All inputs are finite; a program needn't handle non-finite values.
Results may differ from a plain program's by a relative error of at most 0.033.
Values may be sent and summed in bfloat16 or wider, within the bound.
No kernel may reach another device: no remote copies, remote signals or barrier semaphores. Data moves between devices by JAX's collectives and lax.ppermute only.
A program may use at most 64 MiB of HBM per device.

v0:
```python
import math
import jax
import jax.numpy as jnp
import numpy as np
from jax import lax
from jax.sharding import PartitionSpec as P

D = 4096
QUERY_HEAD_COUNT = 32
KEY_VALUE_HEADS = 8
HEAD_SIZE = 128
EXPERTS = 8
TOP = 2
CAP = 16


def slot_table(routes, shard_count, seg_len):
    flat_routes = routes.reshape(shard_count, seg_len * TOP)
    one_hot = (
        flat_routes[:, :, None] == jnp.arange(EXPERTS, dtype=jnp.int32)[None, None, :]
    ).astype(jnp.int32)
    earlier = jnp.cumsum(one_hot, axis=1) - one_hot
    return (jnp.sum(earlier * one_hot, axis=2), jnp.sum(one_hot, axis=1))


def expert_rows(rows_in, w_gate, w_up, w_down):
    gate_val = jnp.dot(rows_in, w_gate, preferred_element_type=jnp.float32)
    up_val = jnp.dot(rows_in, w_up, preferred_element_type=jnp.float32)
    hidden = (jax.nn.silu(gate_val) * up_val).astype(jnp.bfloat16)
    return jnp.dot(hidden, w_down, preferred_element_type=jnp.float32)


def per_device(
    queries, keys, values, out_proj, residual_in, norm_gain, routes, gate_wts, w_gate, w_up, w_down
):
    ctx_count = lax.axis_size("ctx")
    exp_count = lax.axis_size("exp")
    ctx_rank = lax.axis_index("ctx")
    exp_rank = lax.axis_index("exp")
    seg_len = queries.shape[0]
    heads_dev = queries.shape[1] // HEAD_SIZE
    query_group_width = QUERY_HEAD_COUNT // KEY_VALUE_HEADS
    kv_dev = max(1, heads_dev // query_group_width)
    kv_first = exp_rank * heads_dev // query_group_width
    key_part = lax.dynamic_slice_in_dim(keys, kv_first * HEAD_SIZE, kv_dev * HEAD_SIZE, 1)
    value_part = lax.dynamic_slice_in_dim(values, kv_first * HEAD_SIZE, kv_dev * HEAD_SIZE, 1)
    head_map = np.zeros(heads_dev, dtype=np.int32)
    query_pos = ctx_rank * seg_len + jnp.arange(seg_len, dtype=jnp.int32)
    query_heads = queries.reshape(seg_len, heads_dev, HEAD_SIZE)
    score_scale = 1.0 / math.sqrt(HEAD_SIZE)
    run_max = jnp.full((heads_dev, seg_len), -1e30, jnp.float32)
    run_sum = jnp.zeros((heads_dev, seg_len), jnp.float32)
    run_acc = jnp.zeros((heads_dev, seg_len, HEAD_SIZE), jnp.float32)
    key_piece = lax.all_gather(key_part, "ctx", axis=0, tiled=True)
    value_piece = lax.all_gather(value_part, "ctx", axis=0, tiled=True)
    piece_rows = key_piece.shape[0]
    key_heads = key_piece.reshape(piece_rows, kv_dev, HEAD_SIZE)[:, head_map, :]
    value_heads = value_piece.reshape(piece_rows, kv_dev, HEAD_SIZE)[:, head_map, :]
    scores = (
        jnp.einsum("shd,nhd->hsn", query_heads, key_heads, preferred_element_type=jnp.float32)
        * score_scale
    )
    key_pos = jnp.arange(piece_rows, dtype=jnp.int32)
    visible = (query_pos[:, None] >= key_pos[None, :])[None, :, :]
    scores = jnp.where(visible, scores, -1e30)
    new_max = jnp.maximum(run_max, jnp.max(scores, axis=2))
    weights = jnp.where(visible, jnp.exp(scores - new_max[:, :, None]), 0.0)
    factor = jnp.exp(run_max - new_max)
    new_sum = run_sum * factor + jnp.sum(weights, axis=2)
    added = jnp.einsum(
        "hsn,nhd->hsd",
        weights.astype(jnp.bfloat16),
        value_heads,
        preferred_element_type=jnp.float32,
    )
    run_max, run_sum, run_acc = (new_max, new_sum, run_acc * factor[:, :, None] + added)
    attn_local = (
        (run_acc / run_sum[:, :, None])
        .transpose(1, 0, 2)
        .reshape(seg_len, heads_dev * HEAD_SIZE)
        .astype(jnp.bfloat16)
    )
    attn_all = lax.all_gather(attn_local, "exp", axis=1, tiled=True)
    projected = jnp.dot(
        attn_all,
        lax.all_gather(out_proj, "ctx", axis=0, tiled=True),
        preferred_element_type=jnp.float32,
    )
    residual = residual_in.astype(jnp.float32) + projected
    residual_out = residual.astype(jnp.bfloat16)
    sq_mean = lax.psum(jnp.sum(residual * residual, axis=1), "exp") / D
    normed = (residual * lax.rsqrt(sq_mean + 1e-05)[:, None] * norm_gain[None, :]).astype(
        jnp.bfloat16
    )
    quarters = exp_count // EXPERTS
    my_expert = exp_rank // quarters
    slot_all, counts_all = slot_table(routes, ctx_count, seg_len)
    own_slot = lax.dynamic_index_in_dim(slot_all, ctx_rank, 0, keepdims=False).reshape(seg_len, TOP)
    own_route = lax.dynamic_slice_in_dim(routes, ctx_rank * seg_len, seg_len, 0)
    slot_ids = jnp.arange(CAP, dtype=jnp.int32)
    full_rows = lax.all_gather(normed, "exp", axis=1, tiled=True)
    chosen = (
        ((own_route[None, :, :] == my_expert) & (own_slot[None, :, :] == slot_ids[:, None, None]))
        .astype(jnp.int32)
        .sum(axis=2)
        .astype(jnp.bfloat16)
    )
    picked = jnp.dot(chosen, full_rows, preferred_element_type=jnp.float32).astype(jnp.bfloat16)
    rows_all = lax.all_gather(picked, "ctx", axis=0, tiled=True)
    summed = lax.psum_scatter(
        expert_rows(rows_all, w_gate, w_up, w_down).astype(jnp.bfloat16),
        "ctx",
        scatter_dimension=0,
        tiled=True,
    )
    returned = lax.all_to_all(
        summed.reshape(1, CAP, summed.shape[1]), "exp", split_axis=2, concat_axis=0, tiled=True
    )
    owner_expert = jnp.arange(exp_count, dtype=jnp.int32) // quarters
    match_expert = (own_route[:, :, None] == owner_expert[None, None, :]).astype(jnp.float32)
    match_slot = (own_slot[:, :, None] == slot_ids[None, None, :]).astype(jnp.float32)
    combine = jnp.einsum(
        "tk,tkj,tks->tjs", gate_wts, match_expert, match_slot, precision=lax.Precision.HIGHEST
    ).reshape(seg_len, exp_count * CAP)
    flat_returned = returned.reshape(exp_count * CAP, returned.shape[2]).astype(jnp.float32)
    expert_out = jnp.dot(combine, flat_returned, precision=lax.Precision.HIGHEST).astype(
        jnp.bfloat16
    )
    return (residual_out, expert_out)


def solution(mesh):
    placed = (
        P("ctx", "exp"),
        P("ctx", None),
        P("ctx", None),
        P("ctx", "exp"),
        P("ctx", "exp"),
        P("exp"),
        P(),
        P("ctx", None),
        P(None, ("exp", "ctx")),
        P(None, ("exp", "ctx")),
        P(("exp", "ctx"), None),
    )
    return jax.shard_map(
        per_device,
        mesh=mesh,
        in_specs=placed,
        out_specs=(P("ctx", "exp"), P("ctx", "exp")),
        check_vma=False,
    )
```

profile of v0, /device:TPU:1, one launch (start us, length us, event | category | flops | bytes accessed | tf_op | source)
XLA Modules:
  0.0 401.2 jit_solution(1183322907352983559)
XLA Ops:
  8.0 0.9 copy.43
  9.3 2.8 select_reduce_fusion
  12.5 0.8 broadcast_compare_fusion
  13.3 0.7 constant_dynamic-slice_fusion.2
  14.7 31.5 %all_gather.18 = bf16[1024,128]{1,0:T(8,128)(2,1)S(1)} all-gather(bf16[64,128]{1,0:T(8,128)(2,1)S(1)} %constant_dynamic-slice_fusion.2), channel_id=1, replica_groups=mesh['ctx'=16,'exp'=32] {'ctx'}, dimensions={0}, use_global_device_ids=true | all-gather | bytes 278528 | tf_op jit(solution)/shard_map/all_gather | solution.py:54
  46.3 21.8 %all_gather.19 = bf16[1024,128]{1,0:T(8,128)(2,1)S(1)} all-gather(bf16[64,128]{1,0:T(8,128)(2,1)S(1)} %constant_dynamic-slice_fusion.1), channel_id=1, replica_groups=mesh['ctx'=16,'exp'=32] {'ctx'}, dimensions={0}, use_global_device_ids=true | all-gather | bytes 278528 | tf_op jit(solution)/shard_map/all_gather | solution.py:55
  68.9 37.8 %all_gather.20 = bf16[64,4096]{1,0:T(8,128)(2,1)S(1)} all-gather(bf16[64,128]{1,0:T(8,128)(2,1)S(1)} %fusion.8), channel_id=1, replica_groups=mesh['ctx'=16,'exp'=32] {'exp'}, dimensions={1}, use_global_device_ids=true | all-gather | bytes 540672 | tf_op jit(solution)/shard_map/all_gather | solution.py:83
  106.7 1.6 multiply_reduce_fusion
  108.3 62.2 %psum.7 = f32[64]{0:T(128)S(1)} all-reduce(f32[64]{0:T(128)S(1)} %get-tuple-element.10), channel_id=1, replica_groups=mesh['ctx'=16,'exp'=32] {'exp'}, use_global_device_ids=true, to_apply=%region_6.7 | all-reduce | flops 64 | bytes 512 | tf_op jit(solution)/shard_map/psum | solution.py:91
  171.1 25.0 %all_gather.22 = bf16[64,4096]{1,0:T(8,128)(2,1)S(1)} all-gather(bf16[64,128]{1,0:T(8,128)(2,1)S(1)} %get-tuple-element.4), channel_id=1, replica_groups=mesh['ctx'=16,'exp'=32] {'exp'}, dimensions={1}, use_global_device_ids=true | all-gather | bytes 540672 | tf_op jit(solution)/shard_map/all_gather | solution.py:101
  196.1 0.8 convolution_convert_fusion.1
  197.2 59.8 %all-gather.5.cloned.1.call-done = bf16[256,4096]{1,0:T(8,128)(2,1)} async-done(((bf16[16,4096]{1,0:T(8,128)(2,1)}), bf16[256,4096]{1,0:T(8,128)(2,1)}) %all-gather.5.cloned.1.call-update) | async-done | bytes 2097168 | tf_op jit(solution)/shard_map/all_gather | solution.py:109
  257.0 2.7 fusion.37
  259.7 3.9 convolution_convert_fusion
  264.4 68.4 %reduce-scatter.2.cloned.1.call-done = bf16[16,4096]{1,0:T(8,128)(2,1)} async-done(((bf16[256,4096]{1,0:T(8,128)(2,1)}), bf16[16,4096]{1,0:T(8,128)(2,1)}) %reduce-scatter.2.cloned.1.call-update) | async-done | bytes 131088 | tf_op jit(solution)/shard_map/reduce_scatter | solution.py:110
  332.9 4.3 %copy.48 = bf16[1,16,4096]{1,0,2:T(2,128)(2,1)S(1)} copy(bf16[1,16,4096]{2,1,0:T(8,128)(2,1)} %bitcast.36) | data formatting | bytes 262144 | tf_op jit(solution)/shard_map/reshape | solution.py:117
  337.7 23.4 %reduce.6 = bf16[4096,16]{1,0:T(8,128)(2,1)} reduce(bf16[4096,1,16]{2,1,0:T(2,128)(2,1)S(1)} %bitcast.30, bf16[]{:T(256)} %broadcast.104), dimensions={1}, to_apply=%bitcast.14.reduce_sub_computation | reduce | bytes 262146
  361.1 3.1 reshape.120
  364.2 17.9 %all-to-all-start = ((bf16[32,2,1024]{2,1,0:T(2,128)(2,1)}), bf16[32,2,1024]{2,1,0:T(2,128)(2,1)S(1)}, u32[]{:S(2)}, u32[]{:S(2)}) async-start(bf16[32,2,1024]{2,1,0:T(2,128)(2,1)} %reshape.120), calls=%async_computation.1 | async-start | bytes 262144 | tf_op jit(solution)/shard_map/all_to_all | solution.py:116
  382.1 0.9 fusion.21
  383.3 6.5 %all-to-all-done = bf16[32,2,1024]{2,1,0:T(2,128)(2,1)S(1)} async-done(((bf16[32,2,1024]{2,1,0:T(2,128)(2,1)}), bf16[32,2,1024]{2,1,0:T(2,128)(2,1)S(1)}, u32[]{:S(2)}, u32[]{:S(2)}) %all-to-all-start) | async-done | bytes 131104 | tf_op jit(solution)/shard_map/all_to_all | solution.py:116
  389.7 1.8 reshape.121
  391.6 2.0 copy.49
  393.7 1.0 convolution_convert_fusion.2
  (42 shorter events, 5.6 us)
Async XLA Ops:
  7.2 252.6 %copy-start = (bf16[128,4096]{1,0:T(8,128)(2,1)S(1)}, bf16[128,4096]{1,0:T(8,128)(2,1)}, u32[]{:S(2)}) copy-start(bf16[128,4096]{1,0:T(8,128)(2,1)} %param.24) | copy-start | bytes 3145732
  7.2 60.9 %copy-start.3 = (bf16[64,128]{1,0:T(8,128)(2,1)S(1)}, bf16[64,128]{1,0:T(8,128)(2,1)}, u32[]{:S(2)}) copy-start(bf16[64,128]{1,0:T(8,128)(2,1)} %param.14) | copy-start | bytes 49156
  7.2 99.5 %all-gather.3.cloned.1.call-start = ((), (), s32[]{:S(2)}) async-start(), calls=%async_computation.2 | async-start | bytes 1114112 | tf_op jit(solution)/shard_map/all_gather | solution.py:86
  7.9 249.1 %all-gather.5.cloned.1.call-start = ((), (), s32[]{:S(2)}) async-start(), calls=%async_computation.3 | async-start | bytes 2228224 | tf_op jit(solution)/shard_map/all_gather | solution.py:109
  8.0 98.7 %copy-start.2 = (bf16[64,128]{1,0:T(8,128)(2,1)S(1)}, bf16[64,128]{1,0:T(8,128)(2,1)}, u32[]{:S(2)}) copy-start(bf16[64,128]{1,0:T(8,128)(2,1)} %param.18) | copy-start | bytes 49156
  14.7 155.8 %copy-start.5 = (f32[128]{0:T(128)S(1)}, f32[128]{0:T(128)}, u32[]{:S(2)}) copy-start(f32[128]{0:T(128)} %param.19) | copy-start | bytes 1540
  197.0 135.8 %reduce-scatter.2.cloned.1.call-start = ((), (), s32[]{:S(2)}) async-start(), calls=%async_computation.4 | async-start | bytes 2228224 | tf_op jit(solution)/shard_map/reduce_scatter | solution.py:110
  257.0 2.7 copy-start.1
  263.6 0.7 copy-start.4
  364.2 25.5 %all-to-all-start = ((bf16[32,2,1024]{2,1,0:T(2,128)(2,1)}), bf16[32,2,1024]{2,1,0:T(2,128)(2,1)S(1)}, u32[]{:S(2)}, u32[]{:S(2)}) async-start(bf16[32,2,1024]{2,1,0:T(2,128)(2,1)} %reshape.120), calls=%async_computation.1 | async-start | bytes 262144 | tf_op jit(solution)/shard_map/all_to_all | solution.py:116
Sparse Core Ops, SparseCore 0:
  10.1 66.9 all-gather.2
  197.1 59.8 all-gather.4
  263.8 69.0 reduce-scatter.1
where the time goes:
time: 402 us; the launch traced here: 401 us
  blocking collectives  178 us (44%)
  waiting for transfers between devices  135 us (34%)
  other arithmetic  27.9 us (7%)
  starting transfers between devices  18.2 us (5%)
  local copies, waits for them, and re-layouts  16 us (4%)
  between operations  13.9 us (3%)
  matrix products  11.5 us (3%)
    reduce_scatter x1, waiting for transfers between devices, per_device(): lax.psum_scatter(expert_rows(rows_all, w_gate, w_up, w_down).astype(jnp.b...  68.4 us
    psum x1, blocking collectives, per_device(): sq_mean = lax.psum(jnp.sum(residual * residual, axis=1), 'exp') / D  62.2 us
    all_gather x1, waiting for transfers between devices, per_device(): rows_all = lax.all_gather(picked, 'ctx', axis=0, tiled=True)  59.8 us
    all_gather x1, blocking collectives, per_device(): attn_all = lax.all_gather(attn_local, 'exp', axis=1, tiled=True)  37.8 us
    all_gather x1, blocking collectives, per_device(): key_piece = lax.all_gather(key_part, 'ctx', axis=0, tiled=True)  31.5 us
    all_gather x1, blocking collectives, per_device(): full_rows = lax.all_gather(normed, 'exp', axis=1, tiled=True)  25 us
    unnamed x1, other arithmetic  23.4 us
    all_gather x1, blocking collectives, per_device(): value_piece = lax.all_gather(value_part, 'ctx', axis=0, tiled=True)  21.8 us
  transfers between devices with their start and end apart: 4, of which 3 were waited for; matrix products, arithmetic and copies ran while one was open for 2% of the time, Pallas kernels for 0%

commit v1 on v0

--- a/solution.py
+++ b/solution.py
@@ -51,8 +51,11 @@
     run_max = jnp.full((heads_dev, seg_len), -1e30, jnp.float32)
     run_sum = jnp.zeros((heads_dev, seg_len), jnp.float32)
     run_acc = jnp.zeros((heads_dev, seg_len, HEAD_SIZE), jnp.float32)
-    key_piece = lax.all_gather(key_part, "ctx", axis=0, tiled=True)
-    value_piece = lax.all_gather(value_part, "ctx", axis=0, tiled=True)
+    key_piece, value_piece = jnp.split(
+        lax.all_gather(jnp.concatenate([key_part, value_part], axis=1), "ctx", axis=0, tiled=True),
+        [key_part.shape[1]],
+        axis=1,
+    )
     piece_rows = key_piece.shape[0]
     key_heads = key_piece.reshape(piece_rows, kv_dev, HEAD_SIZE)[:, head_map, :]
     value_heads = value_piece.reshape(piece_rows, kv_dev, HEAD_SIZE)[:, head_map, :]

time: 402 us -> 379 us (0.943)
  blocking collectives: 178 us -> 157 us
    all_gather x2 -> x1, blocking collectives: 53.3 us -> 33.2 us  [per_device(): lax.all_gather(jnp.concatenate([key_part, value_part], axis=1), 'ctx', ax...]
    psum x1, blocking collectives: 62.2 us -> 68.2 us  [per_device(): sq_mean = lax.psum(jnp.sum(residual * residual, axis=1), 'exp') / D]
    all_gather x1, blocking collectives: 37.8 us -> 33.1 us  [per_device(): attn_all = lax.all_gather(attn_local, 'exp', axis=1, tiled=True)]
where the time goes in v1:
time: 379 us; the launch traced here: 378 us
  blocking collectives  157 us (41%)
  waiting for transfers between devices  134 us (35%)
  other arithmetic  27.9 us (7%)
  starting transfers between devices  18.3 us (5%)
  local copies, waits for them, and re-layouts  15.3 us (4%)
  between operations  13.9 us (4%)
  matrix products  11.5 us (3%)
    reduce_scatter x1, waiting for transfers between devices, per_device(): lax.psum_scatter(expert_rows(rows_all, w_gate, w_up, w_down).astype(jnp.b...  68.3 us
    psum x1, blocking collectives, per_device(): sq_mean = lax.psum(jnp.sum(residual * residual, axis=1), 'exp') / D  68.2 us
    all_gather x1, waiting for transfers between devices, per_device(): rows_all = lax.all_gather(picked, 'ctx', axis=0, tiled=True)  58.9 us
    all_gather x1, blocking collectives, per_device(): lax.all_gather(jnp.concatenate([key_part, value_part], axis=1), 'ctx', ax...  33.2 us
    all_gather x1, blocking collectives, per_device(): attn_all = lax.all_gather(attn_local, 'exp', axis=1, tiled=True)  33.1 us
    unnamed x1, other arithmetic  23.4 us
    all_gather x1, blocking collectives, per_device(): full_rows = lax.all_gather(normed, 'exp', axis=1, tiled=True)  22.4 us
    all_to_all x1, starting transfers between devices, per_device(): lax.all_to_all(summed.reshape(1, CAP, summed.shape[1]), 'exp', split_axis...  18 us
  transfers between devices with their start and end apart: 4, of which 3 were waited for; matrix products, arithmetic and copies ran while one was open for 2% of the time, Pallas kernels for 0%

profile of v1, /device:TPU:1, one launch (start us, length us, event | category | flops | bytes accessed | tf_op | source)
XLA Modules:
  0.0 378.1 jit_solution(2140738698841987422)
XLA Ops:
  7.2 0.7 all-gather.3.cloned.1.call-update
  8.0 0.9 copy.43
  9.3 2.8 select_reduce_fusion
  12.5 0.8 broadcast_compare_fusion
  13.3 0.7 constant_dynamic-slice_fusion.1
  14.0 33.2 %all_gather.15 = bf16[1024,256]{1,0:T(8,128)(2,1)S(1)} all-gather(bf16[64,256]{1,0:T(8,128)(2,1)S(1)} %pad_maximum_fusion), channel_id=1, replica_groups=mesh['ctx'=16,'exp'=32] {'ctx'}, dimensions={0}, use_global_device_ids=true | all-gather | bytes 557056 | tf_op jit(solution)/shard_map/all_gather | solution.py:55
  48.0 33.1 %all_gather.16 = bf16[64,4096]{1,0:T(8,128)(2,1)S(1)} all-gather(bf16[64,128]{1,0:T(8,128)(2,1)S(1)} %fusion.8), channel_id=1, replica_groups=mesh['ctx'=16,'exp'=32] {'exp'}, dimensions={1}, use_global_device_ids=true | all-gather | bytes 540672 | tf_op jit(solution)/shard_map/all_gather | solution.py:86
  81.1 1.6 multiply_reduce_fusion
  82.8 68.2 %psum.7 = f32[64]{0:T(128)S(1)} all-reduce(f32[64]{0:T(128)S(1)} %get-tuple-element.10), channel_id=1, replica_groups=mesh['ctx'=16,'exp'=32] {'exp'}, use_global_device_ids=true, to_apply=%region_6.7 | all-reduce | flops 64 | bytes 512 | tf_op jit(solution)/shard_map/psum | solution.py:94
  151.6 22.4 %all_gather.18 = bf16[64,4096]{1,0:T(8,128)(2,1)S(1)} all-gather(bf16[64,128]{1,0:T(8,128)(2,1)S(1)} %get-tuple-element.4), channel_id=1, replica_groups=mesh['ctx'=16,'exp'=32] {'exp'}, dimensions={1}, use_global_device_ids=true | all-gather | bytes 540672 | tf_op jit(solution)/shard_map/all_gather | solution.py:104
  174.0 0.8 convolution_convert_fusion.1
  175.1 58.9 %all-gather.5.cloned.1.call-done = bf16[256,4096]{1,0:T(8,128)(2,1)} async-done(((bf16[16,4096]{1,0:T(8,128)(2,1)}), bf16[256,4096]{1,0:T(8,128)(2,1)}) %all-gather.5.cloned.1.call-update) | async-done | bytes 2097168 | tf_op jit(solution)/shard_map/all_gather | solution.py:112
  234.0 2.7 fusion.39
  236.7 3.9 %convolution_convert_fusion = bf16[256,4096]{1,0:T(8,128)(2,1)} fusion(bf16[128,4096]{1,0:T(8,128)(2,1)S(1)} %copy-done, bf16[256,4096]{1,0:T(8,128)(2,1)S(1)} %copy-done.1, bf16[4096,128]{1,0:T(8,128)(2,1)} %param.23, f32[256,128]{1,0:T(8,128)S(1)} %fusion.39), kind=kOutput, calls=%fused_computation | convolution fusion | flops 538116096 | bytes 6422528 | tf_op jit(solution)/shard_map/dot_general | solution.py:30
  241.4 68.3 %reduce-scatter.2.cloned.1.call-done = bf16[16,4096]{1,0:T(8,128)(2,1)} async-done(((bf16[256,4096]{1,0:T(8,128)(2,1)}), bf16[16,4096]{1,0:T(8,128)(2,1)}) %reduce-scatter.2.cloned.1.call-update) | async-done | bytes 131088 | tf_op jit(solution)/shard_map/reduce_scatter | solution.py:113
  309.7 4.3 %copy.48 = bf16[1,16,4096]{1,0,2:T(2,128)(2,1)S(1)} copy(bf16[1,16,4096]{2,1,0:T(8,128)(2,1)} %bitcast.34) | data formatting | bytes 262144 | tf_op jit(solution)/shard_map/reshape | solution.py:120
  314.5 23.4 %reduce.6 = bf16[4096,16]{1,0:T(8,128)(2,1)} reduce(bf16[4096,1,16]{2,1,0:T(2,128)(2,1)S(1)} %bitcast.28, bf16[]{:T(256)} %broadcast.104), dimensions={1}, to_apply=%bitcast.14.reduce_sub_computation | reduce | bytes 262146
  337.9 3.1 reshape.120
  341.0 18.0 %all-to-all-start = ((bf16[32,2,1024]{2,1,0:T(2,128)(2,1)}), bf16[32,2,1024]{2,1,0:T(2,128)(2,1)S(1)}, u32[]{:S(2)}, u32[]{:S(2)}) async-start(bf16[32,2,1024]{2,1,0:T(2,128)(2,1)} %reshape.120), calls=%async_computation.1 | async-start | bytes 262144 | tf_op jit(solution)/shard_map/all_to_all | solution.py:119
  359.1 0.9 fusion.23
  360.2 6.5 %all-to-all-done = bf16[32,2,1024]{2,1,0:T(2,128)(2,1)S(1)} async-done(((bf16[32,2,1024]{2,1,0:T(2,128)(2,1)}), bf16[32,2,1024]{2,1,0:T(2,128)(2,1)S(1)}, u32[]{:S(2)}, u32[]{:S(2)}) %all-to-all-start) | async-done | bytes 131104 | tf_op jit(solution)/shard_map/all_to_all | solution.py:119
  366.7 1.8 reshape.121
  368.5 2.0 copy.49
  370.6 1.0 convolution_convert_fusion.2
  (41 shorter events, 4.2 us)
Async XLA Ops:
  7.2 229.5 %copy-start = (bf16[128,4096]{1,0:T(8,128)(2,1)S(1)}, bf16[128,4096]{1,0:T(8,128)(2,1)}, u32[]{:S(2)}) copy-start(bf16[128,4096]{1,0:T(8,128)(2,1)} %param.24) | copy-start | bytes 3145732
  7.2 40.0 %copy-start.5 = (bf16[64,128]{1,0:T(8,128)(2,1)S(1)}, bf16[64,128]{1,0:T(8,128)(2,1)}, u32[]{:S(2)}) copy-start(bf16[64,128]{1,0:T(8,128)(2,1)} %param.14) | copy-start | bytes 49156
  7.2 74.0 %all-gather.3.cloned.1.call-start = ((), (), s32[]{:S(2)}) async-start(), calls=%async_computation.2 | async-start | bytes 1114112 | tf_op jit(solution)/shard_map/all_gather | solution.py:89
  7.9 226.1 %all-gather.5.cloned.1.call-start = ((), (), s32[]{:S(2)}) async-start(), calls=%async_computation.3 | async-start | bytes 2228224 | tf_op jit(solution)/shard_map/all_gather | solution.py:112
  8.9 72.2 %copy-start.2 = (bf16[64,128]{1,0:T(8,128)(2,1)S(1)}, bf16[64,128]{1,0:T(8,128)(2,1)}, u32[]{:S(2)}) copy-start(bf16[64,128]{1,0:T(8,128)(2,1)} %param.18) | copy-start | bytes 49156
  47.2 103.8 %copy-start.4 = (f32[128]{0:T(128)S(1)}, f32[128]{0:T(128)}, u32[]{:S(2)}) copy-start(f32[128]{0:T(128)} %param.19) | copy-start | bytes 1540
  174.8 134.8 %reduce-scatter.2.cloned.1.call-start = ((), (), s32[]{:S(2)}) async-start(), calls=%async_computation.4 | async-start | bytes 2228224 | tf_op jit(solution)/shard_map/reduce_scatter | solution.py:113
  234.0 2.7 copy-start.1
  240.6 0.7 copy-start.3
  341.0 25.7 %all-to-all-start = ((bf16[32,2,1024]{2,1,0:T(2,128)(2,1)}), bf16[32,2,1024]{2,1,0:T(2,128)(2,1)S(1)}, u32[]{:S(2)}, u32[]{:S(2)}) async-start(bf16[32,2,1024]{2,1,0:T(2,128)(2,1)} %reshape.120), calls=%async_computation.1 | async-start | bytes 262144 | tf_op jit(solution)/shard_map/all_to_all | solution.py:119
Sparse Core Ops, SparseCore 0:
  10.1 66.7 all-gather.2
  175.0 58.9 all-gather.4
  240.8 68.8 reduce-scatter.1
